TPU v7x, 32 devices: a whole 2x2x4 slice. The times are simulated.
32 devices in a mesh: ctx: 4 (over y, x), exp: 8 (over z, core).
Axes of the slice: x: 2, y: 2, z: 4, core: 2. Of those that a mesh axis runs over, the one named last changes fastest.
Arguments:
- tokens: bfloat16 [1024, 4096], P('exp', 'ctx'), may hold values from -6 to 6
- cotangent: bfloat16 [1024, 4096], P('exp', 'ctx'), may hold values from -6 to 6
- routes: int32 [1024, 8], P('exp'), may hold values from 0 to 15, all different within a row; in each aligned block of 128 rows (0 to 127, 128 to 255, ...) at most 96 rows name the same one
- router_weight: float32 [4096, 16], P('ctx'), may hold values from -0.09375 to 0.09375
- expert_out: bfloat16 [16, 768, 4096], P('exp', None, 'ctx'), may hold values from -6 to 6
Outputs:
- mixed: bfloat16 [1024, 4096], P('exp', 'ctx')
- token_grad: bfloat16 [1024, 4096], P('exp', 'ctx')
- router_grad: float32 [4096, 16], P('ctx')
- slot_grad: bfloat16 [16, 768, 4096], P('exp', None, 'ctx')
Inputs may be any that keep to these rules, and one draw needn't show every extreme that they name: `routes`: each row names 8 different experts; among the rows of one index of exp no expert is named more than 96 times.
All inputs are finite; a program needn't handle non-finite values.
Results may differ from a plain program's by a relative error of at most 0.00105.
Values may be sent and summed in bfloat16 or wider, within the bound.
A program may use at most 64 MiB of HBM per device.

v0:
```python
import jax
import jax.numpy as jnp
from jax import lax
from jax.sharding import PartitionSpec as P


def body(tokens, cotangent, routes, router_weight, expert_out):
    rows, top = routes.shape
    local = expert_out.shape[0]
    sources = lax.axis_size("exp")
    experts = local * sources
    capacity = expert_out.shape[1] // sources
    width = tokens.shape[1]
    highest = lax.Precision.HIGHEST
    flat = routes.reshape(-1)
    onehot = (flat[:, None] == jnp.arange(experts, dtype=jnp.int32)[None, :]).astype(jnp.int32)
    earlier = jnp.cumsum(onehot, axis=0) - onehot
    position = jnp.sum(earlier * onehot, axis=1)
    target = flat % local * (sources * capacity) + flat // local * capacity + position
    layout = (local, sources, capacity, width)
    buffer_rows = local * sources * capacity
    tokens_wide = tokens.astype(jnp.float32)
    partial_logits = jnp.dot(tokens_wide, router_weight, precision=highest)
    logits = lax.psum(partial_logits, "ctx")
    expo = jnp.exp(logits)
    probs = expo / jnp.sum(expo, axis=1, keepdims=True)
    chosen = jnp.take_along_axis(probs, routes, axis=1)
    total = jnp.sum(chosen, axis=1, keepdims=True)
    gates = chosen / total
    returned = lax.all_to_all(
        expert_out.reshape(layout), "exp", split_axis=1, concat_axis=1, tiled=True
    )
    pairs = (
        jnp.take(returned.reshape(buffer_rows, width), target, axis=0)
        .reshape(rows, top, width)
        .astype(jnp.float32)
    )
    mixed = jnp.sum(gates[:, :, None] * pairs, axis=1).astype(jnp.bfloat16)
    partial_dots = jnp.sum(cotangent.astype(jnp.float32)[:, None, :] * pairs, axis=2)
    weighted = (
        gates.reshape(-1)[:, None] * jnp.repeat(cotangent, top, axis=0).astype(jnp.float32)
    ).astype(jnp.bfloat16)
    weighted_send = jnp.zeros((buffer_rows, width), jnp.bfloat16).at[target].set(weighted)
    slot_grad = lax.all_to_all(
        weighted_send.reshape(layout), "exp", split_axis=1, concat_axis=1, tiled=True
    )
    slot_grad = slot_grad.reshape(local, sources * capacity, width)
    dots = lax.psum(partial_dots, "ctx")
    dchosen = (dots - jnp.sum(dots * gates, axis=1, keepdims=True)) / total
    match = (routes[:, :, None] == jnp.arange(experts, dtype=jnp.int32)[None, None, :]).astype(
        jnp.float32
    )
    spread = jnp.sum(match * dchosen[:, :, None], axis=1)
    dlogits = probs * (spread - jnp.sum(chosen * dchosen, axis=1, keepdims=True))
    token_grad = jnp.dot(dlogits, router_weight.T, precision=highest).astype(jnp.bfloat16)
    partial_router = jnp.dot(tokens_wide.T, dlogits, precision=highest)
    router_grad = lax.psum(partial_router, "exp")
    return (mixed, token_grad, router_grad, slot_grad)


def solution(mesh):
    in_specs = (
        P("exp", "ctx"),
        P("exp", "ctx"),
        P("exp", None),
        P("ctx", None),
        P("exp", None, "ctx"),
    )
    out_specs = (P("exp", "ctx"), P("exp", "ctx"), P("ctx", None), P("exp", None, "ctx"))
    return jax.shard_map(body, mesh=mesh, in_specs=in_specs, out_specs=out_specs, check_vma=False)
```

profile of v0, /device:TPU:0, one launch (start us, length us, event | category | flops | bytes accessed | tf_op | source)
XLA Modules:
  0.0 223.3 jit_solution(89217931586573706)
XLA Ops:
  7.2 4.0 %copy.85 = bf16[2,8,96,1024]{3,2,0,1:T(8,128)(2,1)} copy(bf16[2,8,96,1024]{3,2,1,0:T(8,128)(2,1)} %bitcast.49) | data formatting | bytes 6291456 | tf_op jit(solution)/shard_map/reshape | solution.py:31
  11.2 6.5 %all-to-all-start = ((bf16[2,8,96,1024]{3,2,0,1:T(8,128)(2,1)}), bf16[2,8,96,1024]{3,2,0,1:T(8,128)(2,1)}, u32[]{:S(2)}, u32[]{:S(2)}) async-start(bf16[2,8,96,1024]{3,2,0,1:T(8,128)(2,1)} %copy.85), calls=%async_computation | async-start | bytes 6291456 | tf_op jit(solution)/shard_map/all_to_all | solution.py:30
  17.7 0.1 copy.79
  17.8 0.1 reshape.243
  18.0 0.1 reshape.239
  18.1 0.1 copy.76
  18.2 0.1 reshape.254
  18.3 4.5 %reduce-window.6 = s32[16,8,128]{2,1,0:T(8,128)S(1)} reduce-window(s32[16,8,128]{2,1,0:T(8,128)S(1)} %fusion.10, s32[]{:T(128)} %constant.60.clone.1), window={size=1x1x128 pad=0_0x0_0x127_0}, to_apply=%region_3.4 | reduce-window | flops 2080768 | bytes 131076 | tf_op jit(solution)/shard_map/reduce-window
  22.9 0.1 copy.81
  23.4 0.1 copy.84
  23.6 0.1 broadcast_in_dim.38
  23.7 0.8 convert_element_type.36
  24.6 0.3 fusion.23
  24.9 0.2 copy-done.7
  25.2 64.1 %all-to-all-done = bf16[2,8,96,1024]{3,2,0,1:T(8,128)(2,1)} async-done(((bf16[2,8,96,1024]{3,2,0,1:T(8,128)(2,1)}), bf16[2,8,96,1024]{3,2,0,1:T(8,128)(2,1)}, u32[]{:S(2)}, u32[]{:S(2)}) %all-to-all-start) | async-done | bytes 3145760 | tf_op jit(solution)/shard_map/all_to_all | solution.py:30
  89.3 2.2 copy.86
  91.5 5.4 %gather_fusion = bf16[1024,1024]{1,0:T(8,128)(2,1)} fusion(bf16[1536,1024]{1,0:T(8,128)(2,1)S(1)} %bitcast.47, s32[1024]{0:T(1024)S(1)} %broadcast_clamp_fusion), kind=kCustom, calls=%fused_computation | custom fusion | bytes 4198400 | tf_op jit(solution)/shard_map/jit(_take)/gather | solution.py:34
  96.9 2.4 %fusion = f32[1024]{0:T(1024)S(1)} fusion(bf16[1024,1024]{1,0:T(8,128)(2,1)} %gather_fusion, f32[128,1024]{1,0:T(8,128)} %convert_element_type.36, pred[1024]{0:T(1024)(128)(4,1)S(1)} %broadcast_in_dim.38), kind=kLoop, calls=%fused_computation.5 | loop fusion | flops 4193280 | bytes 2626560 | tf_op jit(solution)/shard_map/reduce_sum | solution.py:39
  99.5 16.0 %all-reduce = (f32[128,16]{0,1:T(8,128)S(1)}, f32[128,8]{0,1:T(8,128)S(1)}) all-reduce(f32[128,16]{0,1:T(8,128)S(1)} %fusion.23, f32[128,8]{0,1:T(8,128)S(1)} %copy.89), channel_id=1, replica_groups=mesh['ctx'=4,'exp'=8] {'ctx'}, use_global_device_ids=true, to_apply=%region_0.0 | all-reduce | flops 3072 | bytes 24576 | tf_op jit(solution)/shard_map/psum | solution.py:24
  115.5 7.0 %gather_fusion.1 = f32[1024]{0:T(1024)S(1)} fusion(f32[128,16]{0,1:T(8,128)S(1)} %exponential_divide_fusion, s32[1024]{0:T(1024)S(1)} %reshape.254), kind=kCustom, calls=%fused_computation.1 | custom fusion | bytes 16384 | tf_op jit(solution)/shard_map/jit(take_along_axis)/gather | solution.py:27
  122.7 0.6 multiply_reduce_fusion.2
  123.3 0.1 copy.78
  123.4 0.7 div.58
  124.1 7.4 %scatter_custom_fusion = bf16[1536,1024]{1,0:T(8,128)(2,1)S(1)} fusion(s32[1024]{0:T(1024)} %bitcast.55, f32[1024]{0:T(1024)} %div.58, f32[128,1024]{1,0:T(8,128)} %convert_element_type.36, bf16[]{:T(256)} %constant.73.clone.1), kind=kCustom, calls=%fused_computation.8 | custom fusion | flops 2097152 | bytes 3674624 | tf_op jit(solution)/shard_map/scatter | solution.py:43
  131.5 2.0 copy.91
  133.6 4.6 %all-to-all-start.1 = ((bf16[2,8,96,1024]{3,2,0,1:T(8,128)(2,1)}), bf16[2,8,96,1024]{3,2,0,1:T(8,128)(2,1)}, u32[]{:S(2)}, u32[]{:S(2)}) async-start(bf16[2,8,96,1024]{3,2,0,1:T(8,128)(2,1)} %copy.91), calls=%async_computation.1 | async-start | bytes 6291456 | tf_op jit(solution)/shard_map/all_to_all | solution.py:44
  138.3 0.9 convolution_bitcast_fusion
  139.2 2.2 multiply_reduce_fusion
  141.4 1.3 convolution_convert_fusion
  142.8 68.2 %all-to-all-done.1 = bf16[2,8,96,1024]{3,2,0,1:T(8,128)(2,1)} async-done(((bf16[2,8,96,1024]{3,2,0,1:T(8,128)(2,1)}), bf16[2,8,96,1024]{3,2,0,1:T(8,128)(2,1)}, u32[]{:S(2)}, u32[]{:S(2)}) %all-to-all-start.1) | async-done | bytes 3145760 | tf_op jit(solution)/shard_map/all_to_all | solution.py:44
  211.0 4.0 %copy.92 = bf16[2,8,96,1024]{3,2,1,0:T(8,128)(2,1)} copy(bf16[2,8,96,1024]{3,2,0,1:T(8,128)(2,1)} %all-to-all-done.1) | data formatting | bytes 6291456 | tf_op jit(solution)/shard_map/all_to_all | solution.py:44
  215.0 1.5 copy.96
  (51 shorter events, 1.1 us)
Async XLA Ops:
  7.2 17.4 %copy-start = (bf16[128,1024]{1,0:T(8,128)(2,1)S(1)}, bf16[128,1024]{1,0:T(8,128)(2,1)}, u32[]{:S(2)}) copy-start(bf16[128,1024]{1,0:T(8,128)(2,1)} %param.5) | copy-start | bytes 786436
  11.2 6.5 %copy-start.4 = (s32[128,8]{0,1:T(8,128)S(1)}, s32[128,8]{0,1:T(8,128)}, u32[]{:S(2)}) copy-start(s32[128,8]{0,1:T(8,128)} %param.7) | copy-start | bytes 12292
  11.2 12.5 %copy-start.2 = (bf16[128,1024]{1,0:T(8,128)(2,1)S(1)}, bf16[128,1024]{1,0:T(8,128)(2,1)}, u32[]{:S(2)}) copy-start(bf16[128,1024]{1,0:T(8,128)(2,1)} %param.6) | copy-start | bytes 786436
  11.2 13.4 %copy-start.3 = (f32[1024,16]{0,1:T(8,128)S(1)}, f32[1024,16]{0,1:T(8,128)}, u32[]{:S(2)}) copy-start(f32[1024,16]{0,1:T(8,128)} %param.8) | copy-start | bytes 196612
  11.2 78.1 %all-to-all-start = ((bf16[2,8,96,1024]{3,2,0,1:T(8,128)(2,1)}), bf16[2,8,96,1024]{3,2,0,1:T(8,128)(2,1)}, u32[]{:S(2)}, u32[]{:S(2)}) async-start(bf16[2,8,96,1024]{3,2,0,1:T(8,128)(2,1)} %copy.85), calls=%async_computation | async-start | bytes 6291456 | tf_op jit(solution)/shard_map/all_to_all | solution.py:30
  23.5 1.4 copy-start.5
  24.6 0.6 copy-start.7
  115.5 7.2 %copy-start.8 = (f32[128,8]{0,1:T(8,128)}, f32[128,8]{0,1:T(8,128)S(1)}, u32[]{:S(2)}) copy-start(f32[128,8]{0,1:T(8,128)S(1)} %get-tuple-element.5) | copy-start | bytes 12292
  122.7 0.6 copy-start.10
  133.5 4.7 %copy-start.9 = (f32[128,8]{0,1:T(8,128)S(1)}, f32[128,8]{0,1:T(8,128)}, u32[]{:S(2)}) copy-start(f32[128,8]{0,1:T(8,128)} %copy-done.8) | copy-start | bytes 12292
  133.5 4.7 %copy-start.11 = (f32[128]{0:T(128)S(1)}, f32[128]{0:T(128)}, u32[]{:S(2)}) copy-start(f32[128]{0:T(128)} %copy-done.10) | copy-start | bytes 1540
  133.5 4.7 %copy-start.12 = (f32[128]{0:T(128)S(1)}, f32[128]{0:T(128)}, u32[]{:S(2)}) copy-start(f32[128]{0:T(128)} %get-tuple-element.8) | copy-start | bytes 1540
  133.5 5.6 %copy-start.1 = (bf16[1024,1024]{1,0:T(8,128)(2,1)S(1)}, bf16[1024,1024]{1,0:T(8,128)(2,1)}, u32[]{:S(2)}) copy-start(bf16[1024,1024]{1,0:T(8,128)(2,1)} %gather_fusion) | copy-start | bytes 6291460
  133.6 5.6 %copy-start.6 = (pred[128,8]{1,0:T(8,128)(4,1)S(1)}, pred[128,8]{1,0:T(8,128)(4,1)}, u32[]{:S(2)}) copy-start(pred[128,8]{1,0:T(8,128)(4,1)} %copy-done.5) | copy-start | bytes 3076
  133.6 77.4 %all-to-all-start.1 = ((bf16[2,8,96,1024]{3,2,0,1:T(8,128)(2,1)}), bf16[2,8,96,1024]{3,2,0,1:T(8,128)(2,1)}, u32[]{:S(2)}, u32[]{:S(2)}) async-start(bf16[2,8,96,1024]{3,2,0,1:T(8,128)(2,1)} %copy.91), calls=%async_computation.1 | async-start | bytes 6291456 | tf_op jit(solution)/shard_map/all_to_all | solution.py:44
  138.2 76.8 %all-reduce.3.cloned.1.call-start = ((), (), s32[]{:S(2)}) async-start(), calls=%async_computation.2 | async-start | bytes 131072 | tf_op jit(solution)/shard_map/psum | solution.py:57
Sparse Core Ops, SparseCore 0:
  141.9 67.8 all-reduce.2
where the time goes:
time: 224 us; the launch traced here: 223 us
  waiting for transfers between devices  132 us (59%)
  local copies, waits for them, and re-layouts  28.6 us (13%)
  other arithmetic  18.4 us (8%)
  blocking collectives  16 us (7%)
  between operations  14.3 us (6%)
  starting transfers between devices  11.1 us (5%)
  matrix products  2.49 us (1%)
    all_to_all x1, waiting for transfers between devices, body(): lax.all_to_all(weighted_send.reshape(layout), 'exp', split_axis=1, concat...  68.2 us
    all_to_all x1, waiting for transfers between devices, body(): lax.all_to_all(expert_out.reshape(layout), 'exp', split_axis=1, concat_ax...  64.1 us
    psum x1, blocking collectives, body(): logits = lax.psum(partial_logits, 'ctx')  16 us
    scatter x1, other arithmetic, body(): jnp.zeros((buffer_rows, width), jnp.bfloat16).at[target].set(weighted)  7.43 us
    gather x5, local copies, waits for them, and re-layouts, body(): chosen = jnp.take_along_axis(probs, routes, axis=1)  7.34 us
    all_to_all x1, starting transfers between devices, body(): lax.all_to_all(expert_out.reshape(layout), 'exp', split_axis=1, concat_ax...  6.46 us
    gather x1, local copies, waits for them, and re-layouts, body(): jnp.take(returned.reshape(buffer_rows, width), target, axis=0)  5.36 us
    another operation x3, other arithmetic  4.64 us
  transfers between devices with their start and end apart: 3, of which 2 were waited for; matrix products, arithmetic and copies ran while one was open for 7% of the time, Pallas kernels for 0%

commit v1 on v0

v1 whole, which is shorter than its diff:
```python
import jax
import jax.numpy as jnp
from jax import lax
from jax.sharding import PartitionSpec as P

HIGHEST = lax.Precision.HIGHEST


def route_slots(routes, experts):
    rows = routes.shape[0]
    match = routes[:, :, None] == jnp.arange(experts, dtype=jnp.int32)[None, None, :]
    mask = jnp.sum(match.astype(jnp.float32), axis=1)
    earlier = jnp.arange(rows)[:, None] > jnp.arange(rows)[None, :]
    slot = jnp.dot(
        earlier.astype(jnp.bfloat16), mask.astype(jnp.bfloat16), preferred_element_type=jnp.float32
    )
    return mask, jnp.where(mask > 0, slot, -1.0)


def body(tokens, cotangent, routes, router_weight, expert_out):
    rows, width = tokens.shape
    local = expert_out.shape[0]
    sources = lax.axis_size("exp")
    experts = local * sources
    capacity = expert_out.shape[1] // sources
    mask, slot = route_slots(routes, experts)
    cot_all = lax.all_gather(cotangent, "exp")
    tokens_wide = tokens.astype(jnp.float32)
    logits = lax.psum(jnp.dot(tokens_wide, router_weight, precision=HIGHEST), "ctx")
    expo = jnp.exp(logits)
    probs = expo / jnp.sum(expo, axis=1, keepdims=True)
    chosen = probs * mask
    total = jnp.sum(chosen, axis=1, keepdims=True)
    gates = chosen / total
    both = jnp.stack([slot.T, gates.T], axis=1).reshape(sources, local, 2, rows)
    both = lax.all_to_all(both, "exp", split_axis=0, concat_axis=0, tiled=True)
    their_slot, their_gate = both[:, :, 0], both[:, :, 1]
    hot = their_slot[:, :, None, :] == jnp.arange(capacity, dtype=jnp.float32)[:, None]
    gathered = jnp.einsum(
        "slct,stw->slcw", hot.astype(jnp.bfloat16), cot_all, preferred_element_type=jnp.float32
    )
    weight = jnp.where(hot, their_gate[:, :, None, :], 0.0)
    slot_gate = jnp.sum(weight, axis=3)
    layout = (local, sources, capacity, width)
    out = jnp.swapaxes(expert_out.reshape(layout), 0, 1).astype(jnp.float32)
    slot_grad = (slot_gate[..., None] * gathered).astype(jnp.bfloat16)
    slot_grad = jnp.swapaxes(slot_grad, 0, 1).reshape(expert_out.shape)
    slot_dots = jnp.sum(gathered * out, axis=3)
    token_dots = jnp.sum(jnp.where(hot, slot_dots[..., None], 0.0), axis=2)
    token_dots = lax.all_to_all(token_dots, "exp", split_axis=0, concat_axis=0, tiled=True)
    dots = lax.psum(token_dots.reshape(experts, rows), "ctx").T
    partial = jnp.einsum("slct,slcw->stw", weight, out, precision=HIGHEST)
    mixed = lax.psum_scatter(partial, "exp", scatter_dimension=0, tiled=False)
    mixed = mixed.astype(jnp.bfloat16)
    dchosen = mask * (dots - jnp.sum(dots * gates, axis=1, keepdims=True)) / total
    dlogits = probs * (dchosen - jnp.sum(chosen * dchosen, axis=1, keepdims=True))
    token_grad = jnp.dot(dlogits, router_weight.T, precision=HIGHEST).astype(jnp.bfloat16)
    router_grad = lax.psum(jnp.dot(tokens_wide.T, dlogits, precision=HIGHEST), "exp")
    return mixed, token_grad, router_grad, slot_grad


def solution(mesh):
    in_specs = (
        P("exp", "ctx"),
        P("exp", "ctx"),
        P("exp", None),
        P("ctx", None),
        P("exp", None, "ctx"),
    )
    out_specs = (P("exp", "ctx"), P("exp", "ctx"), P("ctx", None), P("exp", None, "ctx"))
    return jax.shard_map(body, mesh=mesh, in_specs=in_specs, out_specs=out_specs, check_vma=False)
```

time: 224 us -> 157 us (0.70)
  waiting for transfers between devices: 132 us -> 82.2 us
  local copies, waits for them, and re-layouts: 28.6 us -> 3.66 us
  blocking collectives: 16 us -> 32 us
  matrix products: 2.49 us -> 14.6 us
  other arithmetic: 18.4 us -> 6.69 us
  starting transfers between devices: 11.1 us -> 3.45 us
    all_to_all x2 -> x1, waiting for transfers between devices: 132 us -> 0.34 us  [body(): lax.all_to_all(token_dots, 'exp', split_axis=0, concat_axis=0, tiled=True)]
    psum x1, waiting for transfers between devices: 0.01 us -> 52.9 us  [body(): lax.psum(jnp.dot(tokens_wide.T, dlogits, precision=HIGHEST), 'exp')]
    reduce_scatter x0 -> x1, waiting for transfers between devices: none -> 24.2 us  [body(): mixed = lax.psum_scatter(partial, 'exp', scatter_dimension=0, tiled=False)]
    gather x6 -> x0, local copies, waits for them, and re-layouts: 12.7 us -> none  [the longest x5 7.34 us: body(): chosen = jnp.take_along_axis(probs, routes, axis=1)]
    dot_general x3 -> x6, matrix products: 2.49 us -> 14.6 us  [the longest x1 5.84 us: body(): partial = jnp.einsum('slct,slcw->stw', weight, out, precision=HIGHEST)]
    all_to_all x0 -> x1, blocking collectives: none -> 10.5 us  [body(): both = lax.all_to_all(both, 'exp', split_axis=0, concat_axis=0, tiled=True)]
    all_to_all x2 -> x1, starting transfers between devices: 11.1 us -> 3.33 us  [body(): lax.all_to_all(token_dots, 'exp', split_axis=0, concat_axis=0, tiled=True)]
    scatter x1 -> x0, other arithmetic: 7.43 us -> none  [body(): jnp.zeros((buffer_rows, width), jnp.bfloat16).at[target].set(weighted)]
  transfers between devices with their start and end apart: 3 -> 4, of which waited for: 2 -> 4; matrix products, arithmetic and copies ran while one was open for 7% -> 15% of each run, Pallas kernels for 0% -> 0%
where the time goes in v1:
time: 157 us; the launch traced here: 156 us
  waiting for transfers between devices  82.2 us (52%)
  blocking collectives  32 us (20%)
  matrix products  14.6 us (9%)
  between operations  13.8 us (9%)
  other arithmetic  6.69 us (4%)
  local copies, waits for them, and re-layouts  3.66 us (2%)
  starting transfers between devices  3.45 us (2%)
    psum x1, waiting for transfers between devices, body(): lax.psum(jnp.dot(tokens_wide.T, dlogits, precision=HIGHEST), 'exp')  52.9 us
    reduce_scatter x1, waiting for transfers between devices, body(): mixed = lax.psum_scatter(partial, 'exp', scatter_dimension=0, tiled=False)  24.2 us
    psum x1, blocking collectives, body(): lax.psum(jnp.dot(tokens_wide, router_weight, precision=HIGHEST), 'ctx')  11.5 us
    all_to_all x1, blocking collectives, body(): both = lax.all_to_all(both, 'exp', split_axis=0, concat_axis=0, tiled=True)  10.5 us
    psum x1, blocking collectives, body(): dots = lax.psum(token_dots.reshape(experts, rows), 'ctx').T  9.97 us
    dot_general x1, matrix products, body(): partial = jnp.einsum('slct,slcw->stw', weight, out, precision=HIGHEST)  5.84 us
    dot_general x1, matrix products, body(): jnp.einsum('slct,stw->slcw', hot.astype(jnp.bfloat16), cot_all, preferred...  5.24 us
    all_gather x1, waiting for transfers between devices, body(): cot_all = lax.all_gather(cotangent, 'exp')  4.07 us
  transfers between devices with their start and end apart: 4, of which 4 were waited for; matrix products, arithmetic and copies ran while one was open for 15% of the time, Pallas kernels for 0%

profile of v1, /device:TPU:0, one launch (start us, length us, event | category | flops | bytes accessed | tf_op | source)
XLA Modules:
  0.0 156.4 jit_solution(11085306673902328315)
XLA Ops:
  7.2 0.0 copy-start
  7.2 0.0 all-gather.3.cloned.1.call-start
  7.2 0.7 all-gather.3.cloned.1.call-update
  7.9 0.0 reduce-scatter.2.cloned.1.call-start
  8.0 0.2 copy-done
  8.1 1.1 fusion.18
  9.3 11.5 %psum.21 = f32[128,16]{0,1:T(8,128)S(1)} all-reduce(f32[128,16]{0,1:T(8,128)S(1)} %fusion.18), channel_id=1, replica_groups=mesh['ctx'=4,'exp'=8] {'ctx'}, use_global_device_ids=true, to_apply=%region_1.2 | all-reduce | flops 2048 | bytes 16384 | tf_op jit(solution)/shard_map/psum | solution.py:29
  20.8 0.7 convert_reduce_fusion
  21.5 0.1 convolution_select_fusion
  21.7 10.5 %all_to_all.10 = f32[8,2,2,128]{3,1,2,0:T(2,128)S(1)} all-to-all(f32[8,2,2,128]{3,1,2,0:T(2,128)S(1)} %pad_maximum_fusion), channel_id=1, replica_groups=mesh['ctx'=4,'exp'=8] {'exp'}, dimensions={0} | all-to-all | bytes 32768 | tf_op jit(solution)/shard_map/all_to_all | solution.py:36
  32.2 5.8 %fusion.4 = f32[8,128,1024]{2,1,0:T(8,128)} fusion(bf16[2,8,96,1024]{3,2,1,0:T(8,128)(2,1)} %bitcast.47, f32[8,2,128]{2,1,0:T(2,128)S(1)} %get-tuple-element.11, f32[8,2,128]{2,1,0:T(2,128)S(1)} %get-tuple-element.10), kind=kOutput, calls=%fused_computation.6 | convolution fusion | flops 2416312320 | bytes 7356416 | tf_op jit(solution)/shard_map/slct,slcw->stw/dot_general | solution.py:52
  38.0 0.0 copy-start.1
  38.0 0.0 reduce-scatter.2.cloned.1.call-update
  38.1 4.1 %all-gather.3.cloned.1.call-done = bf16[1024,1024]{1,0:T(8,128)(2,1)} async-done(((bf16[128,1024]{1,0:T(8,128)(2,1)}), bf16[1024,1024]{1,0:T(8,128)(2,1)}) %all-gather.3.cloned.1.call-update) | async-done | bytes 2097168 | tf_op jit(solution)/shard_map/all_gather | solution.py:27
  42.1 0.0 copy-done.1
  42.1 5.2 %multiply_reduce_fusion = (f32[8,2,96]{2,1,0:T(2,128)S(1)}, f32[8,2,96,1024]{3,2,1,0:T(8,128)}) fusion(bf16[2,8,96,1024]{3,2,1,0:T(8,128)(2,1)S(1)} %bitcast.48, bf16[8,128,1024,1]{2,1,3,0:T(8,128)(2,1)} %bitcast.50, f32[8,2,128]{2,1,0:T(2,128)S(1)} %get-tuple-element.10), kind=kOutput, calls=%fused_computation.2 | convolution fusion | flops 407566848 | bytes 11548672 | tf_op jit(solution)/shard_map/slct,stw->slcw/dot_general | solution.py:39
  47.4 0.9 select_reduce_fusion
  48.3 3.3 %all-to-all-start.1 = ((f32[8,2,128]{2,1,0:T(2,128)}), f32[8,2,128]{2,1,0:T(2,128)S(1)}, u32[]{:S(2)}, u32[]{:S(2)}) async-start(f32[8,2,128]{2,1,0:T(2,128)} %get-tuple-element.5), calls=%async_computation.2 | async-start | bytes 16384 | tf_op jit(solution)/shard_map/all_to_all | solution.py:50
  51.6 0.0 all-reduce.2.cloned.1.call-start
  51.7 3.2 %fusion = bf16[2,8,96,1024]{3,2,0,1:T(8,128)(2,1)S(1)} fusion(f32[8,2,96,1024]{3,2,1,0:T(8,128)} %get-tuple-element.13, f32[2,8,96]{2,0,1:T(2,128)S(1)} %bitcast.53), kind=kLoop, calls=%fused_computation.1 | loop fusion | flops 3145728 | bytes 9443328 | tf_op jit(solution)/shard_map/convert_element_type | solution.py:46
  54.9 0.0 copy-start.2
  54.9 2.0 %copy.21 = bf16[2,8,96,1024]{3,2,1,0:T(8,128)(2,1)} copy(bf16[2,8,96,1024]{3,2,0,1:T(8,128)(2,1)S(1)} %fusion) | data formatting | bytes 6291456 | tf_op jit(solution)/shard_map/convert_element_type | solution.py:46
  56.9 0.3 all-to-all-done.1
  57.2 10.0 %psum.22 = f32[128,16]{0,1:T(8,128)S(1)} all-reduce(f32[128,16]{0,1:T(8,128)S(1)} %bitcast.51), channel_id=1, replica_groups=mesh['ctx'=4,'exp'=8] {'ctx'}, use_global_device_ids=true, to_apply=%region_7.8 | all-reduce | flops 2048 | bytes 16384 | tf_op jit(solution)/shard_map/psum | solution.py:51
  67.3 0.9 convolution_bitcast_fusion
  68.1 0.0 copy-done.2
  68.1 1.3 convolution_convert_fusion
  69.5 0.0 all-reduce.2.cloned.1.call-update
  69.5 24.2 %reduce-scatter.2.cloned.1.call-done = f32[1,128,1024]{2,1,0:T(8,128)} async-done(((f32[8,128,1024]{2,1,0:T(8,128)}), f32[1,128,1024]{2,1,0:T(8,128)}) %reduce-scatter.2.cloned.1.call-update) | async-done | bytes 524304 | tf_op jit(solution)/shard_map/reduce_scatter | solution.py:53
  93.7 1.8 %convert_bitcast_fusion = bf16[128,1024]{1,0:T(8,128)(2,1)} fusion(f32[1,128,1024]{2,1,0:T(8,128)} %reduce-scatter.2.cloned.1.call-done), kind=kLoop, calls=%fused_computation.19 | loop fusion | flops 131072 | bytes 786432 | tf_op jit(solution)/shard_map/convert_element_type | solution.py:54
  95.5 52.9 %all-reduce.2.cloned.1.call-done = f32[1024,16]{0,1:T(8,128)} async-done(((f32[1024,16]{0,1:T(8,128)}), f32[1024,16]{0,1:T(8,128)}) %all-reduce.2.cloned.1.call-update) | async-done | bytes 65552 | tf_op jit(solution)/shard_map/psum | solution.py:58
  148.4 1.5 copy.32
  (7 shorter events, 0.1 us)
Async XLA Ops:
  7.2 1.0 copy-start
  7.2 35.0 %all-gather.3.cloned.1.call-start = ((), (), s32[]{:S(2)}) async-start(), calls=%async_computation.5 | async-start | bytes 2359296 | tf_op jit(solution)/shard_map/all_gather | solution.py:27
  7.9 85.8 %reduce-scatter.2.cloned.1.call-start = ((), (), s32[]{:S(2)}) async-start(), calls=%async_computation.3 | async-start | bytes 4718592 | tf_op jit(solution)/shard_map/reduce_scatter | solution.py:53
  38.0 4.1 %copy-start.1 = (bf16[2,768,1024]{2,1,0:T(8,128)(2,1)S(1)}, bf16[2,768,1024]{2,1,0:T(8,128)(2,1)}, u32[]{:S(2)}) copy-start(bf16[2,768,1024]{2,1,0:T(8,128)(2,1)} %param.9) | copy-start | bytes 9437188
  48.3 8.9 %all-to-all-start.1 = ((f32[8,2,128]{2,1,0:T(2,128)}), f32[8,2,128]{2,1,0:T(2,128)S(1)}, u32[]{:S(2)}, u32[]{:S(2)}) async-start(f32[8,2,128]{2,1,0:T(2,128)} %get-tuple-element.5), calls=%async_computation.2 | async-start | bytes 16384 | tf_op jit(solution)/shard_map/all_to_all | solution.py:50
  51.6 96.7 %all-reduce.2.cloned.1.call-start = ((), (), s32[]{:S(2)}) async-start(), calls=%async_computation.4 | async-start | bytes 131072 | tf_op jit(solution)/shard_map/psum | solution.py:58
  54.9 13.2 %copy-start.2 = (f32[1024,16]{0,1:T(8,128)S(1)}, f32[1024,16]{0,1:T(8,128)}, u32[]{:S(2)}) copy-start(f32[1024,16]{0,1:T(8,128)} %param.8) | copy-start | bytes 196612
Sparse Core Ops, SparseCore 0:
  9.6 32.4 all-gather.2
  44.4 49.2 reduce-scatter.1
  96.6 51.7 all-reduce.1

commit v2 on v1

--- a/solution.py
+++ b/solution.py
@@ -1,9 +1,15 @@
+import functools
+
 import jax
 import jax.numpy as jnp
 from jax import lax
+from jax.experimental import pallas as pl
+from jax.experimental.pallas import tpu as pltpu
 from jax.sharding import PartitionSpec as P
 
 HIGHEST = lax.Precision.HIGHEST
+MESH = pl.DeviceIdType.MESH
+F32, BF16 = jnp.float32, jnp.bfloat16
 
 
 def route_slots(routes, experts):
@@ -59,7 +65,373 @@
     return mixed, token_grad, router_grad, slot_grad
 
 
+def dot(a, b, ca, cb, precision=None):
+    return lax.dot_general(
+        a, b, (((ca,), (cb,)), ((), ())), precision=precision, preferred_element_type=F32
+    )
+
+
+def kernel(
+    n_ctx, sources, tokens, cot, routes, weight, out,
+    mixed, token_grad, router_grad, slot_grad,
+    cot_all, acc, give, sib, inc, logit, info_out, info, dots_out, dots_in, dots, rg_out, rg_in,
+    rg_all, ag_send, ag_recv, sib_send, sib_recv, line_send, line_recv, ctx_send, ctx_recv,
+    exp_send, exp_recv,
+):
+    rows, width = tokens.shape
+    local, _, capacity, _ = out.shape
+    experts = local * sources
+    chips = sources // 2
+    last = chips - 1
+    me, my_ctx = lax.axis_index("exp"), lax.axis_index("ctx")
+    z, core = me // 2, lax.rem(me, 2)
+    other = 1 - core
+    sibling = 2 * z + other
+    exp_peers = [lax.rem(me + d, sources) for d in range(1, sources)]
+    ctx_peers = [lax.rem(my_ctx + d, n_ctx) for d in range(1, n_ctx)]
+
+    barrier = pltpu.get_barrier_semaphore()
+    for p in exp_peers:
+        pl.semaphore_signal(barrier, inc=1, device_id={"exp": p}, device_id_type=MESH)
+    for p in ctx_peers:
+        pl.semaphore_signal(barrier, inc=1, device_id={"ctx": p}, device_id_type=MESH)
+    pl.semaphore_wait(barrier, len(exp_peers) + len(ctx_peers))
+
+    def remote(src, dst, send, recv, **to):
+        return pltpu.make_async_remote_copy(
+            src_ref=src, dst_ref=dst, send_sem=send, recv_sem=recv,
+            device_id=to, device_id_type=MESH,
+        )
+
+    def gather(kind, block, to):
+        src = cot if kind == "own" else cot_all.at[block]
+        return lambda way: remote(
+            src, cot_all.at[block], ag_send.at[way, block], ag_recv.at[block], exp=to
+        )
+
+    right, left = me + 2, me - 2
+
+    @pl.when(z < last)
+    def _():
+        gather("own", me, right)(0).start()
+
+    @pl.when(z > 0)
+    def _():
+        gather("own", me, left)(1).start()
+
+    gather("own", me, sibling)(2).start()
+
+    def to_ctx(step, buf):
+        return [
+            remote(buf.at[my_ctx], buf.at[my_ctx], ctx_send.at[step, d], ctx_recv.at[step, my_ctx], ctx=p)
+            for d, p in enumerate(ctx_peers)
+        ], [
+            remote(buf.at[p], buf.at[p], ctx_send.at[step, d], ctx_recv.at[step, p], ctx=p)
+            for d, p in enumerate(ctx_peers)
+        ]
+
+    def to_exp(step, src, dst, gathers=False):
+        return [
+            remote(src if gathers else src.at[p], dst.at[me], exp_send.at[step, d], exp_recv.at[step, me], exp=p)
+            for d, p in enumerate(exp_peers)
+        ], [
+            remote(dst.at[p], dst.at[p], exp_send.at[step, d], exp_recv.at[step, p], exp=p)
+            for d, p in enumerate(exp_peers)
+        ]
+
+    def start(pair):
+        for c in pair[0]:
+            c.start()
+
+    def finish(pair):
+        for c in pair[1]:
+            c.wait_recv()
+        for c in pair[0]:
+            c.wait_send()
+
+    wide = tokens[...].astype(F32)
+    logit[my_ctx] = dot(weight[...], wide, 1, 1, HIGHEST)
+    swap = to_ctx(0, logit)
+    start(swap)
+    expert = lax.broadcasted_iota(jnp.int32, (experts, rows), 0)
+    mask = jnp.zeros((experts, rows), F32)
+    for k in range(routes.shape[0]):
+        mask += jnp.where(expert == routes[k : k + 1, :], 1.0, 0.0)
+    before = lax.broadcasted_iota(jnp.int32, (rows, rows), 0) < lax.broadcasted_iota(
+        jnp.int32, (rows, rows), 1
+    )
+    slot = dot(mask.astype(BF16), jnp.where(before, 1.0, 0.0).astype(BF16), 1, 0)
+    slot = jnp.where(mask > 0, slot, -1.0)
+    finish(swap)
+    expo = jnp.exp(sum(logit[i] for i in range(1, n_ctx)) + logit[0])
+    probs = expo / jnp.sum(expo, axis=0, keepdims=True)
+    chosen = probs * mask
+    total = jnp.sum(chosen, axis=0, keepdims=True)
+    gates = chosen / total
+    for p in range(sources):
+        info_out[p, 0:local] = slot[p * local : (p + 1) * local]
+        info_out[p, local : 2 * local] = gates[p * local : (p + 1) * local]
+    swap = to_exp(0, info_out, info)
+    start(swap)
+    info[me] = info_out[me]
+    finish(swap)
+
+    capacity_iota = lax.broadcasted_iota(jnp.int32, (capacity, rows), 0).astype(F32)
+
+    def part(source):
+        tile = info[source]
+        total = None
+        for i in range(local):
+            gate = tile[local + i : local + i + 1, :]
+            rows_of = out[i, source]
+            hot = capacity_iota == tile[i : i + 1, :]
+            for _ in range(3):
+                piece = gate.astype(BF16)
+                gate = gate - piece.astype(F32)
+                put = jnp.where(hot, piece.astype(F32), 0.0).astype(BF16)
+                term = dot(put, rows_of, 0, 0)
+                total = term if total is None else total + term
+        return total
+
+    def aim(i):
+        return jnp.where(2 * z < chips, last - i, i)
+
+    def to_sibling(chip):
+        return remote(give.at[chip], sib.at[chip], sib_send.at[chip], sib_recv.at[chip], exp=sibling)
+
+    def along(chip, step):
+        to = me + 2 * step
+        place = jnp.where((step < 0) & (z - 1 == chip), chips, chip)
+        return remote(acc.at[chip], inc.at[place], line_send.at[chip], line_recv.at[place], exp=to)
+
+    def arrived(place):
+        remote(inc.at[place], inc.at[place], line_send.at[0], line_recv.at[place], exp=sibling).wait_recv()
+
+    def give_away(i, _):
+        chip = aim(i)
+        give[chip] = part(2 * chip + other)
+        to_sibling(chip).start()
+        return _
+
+    lax.fori_loop(0, chips, give_away, 0)
+
+    def keep(i, _):
+        chip = aim(i)
+        mine = part(2 * chip + core)
+        to_sibling(chip).wait_recv()
+        acc[chip] = mine + sib[chip]
+
+        @pl.when((z == 0) & (chip > z))
+        def _():
+            along(chip, 1).start()
+
+        @pl.when((z == last) & (chip < z))
+        def _():
+            along(chip, -1).start()
+
+        return _
+
+    def keep_loop(i, carry):
+        keep(i, 0)
+        return carry
+
+    lax.fori_loop(0, chips, keep_loop, 0)
+
+    for d in range(1, chips):
+
+        @pl.when(z >= d)
+        def _(d=d):
+            block = me - 2 * d
+            gather("held", block, sibling)(2).wait_recv()
+
+            @pl.when(z < last)
+            def _():
+                gather("held", block, right)(0).start()
+
+            gather("held", block, sibling)(2).start()
+
+        @pl.when(z + d <= last)
+        def _(d=d):
+            block = me + 2 * d
+            gather("held", block, sibling)(2).wait_recv()
+
+            @pl.when(z > 0)
+            def _():
+                gather("held", block, left)(1).start()
+
+            gather("held", block, sibling)(2).start()
+
+    cot_all[me] = cot[...]
+
+    def backward(source, carry):
+        @pl.when(lax.rem(source, 2) != core)
+        def _():
+            gather("held", source, sibling)(2).wait_recv()
+
+        tile = info[source]
+        for i in range(local):
+            hot = capacity_iota == tile[i : i + 1, :]
+            held = dot(jnp.where(hot, 1.0, 0.0).astype(BF16), cot_all[source], 1, 0)
+            gate = jnp.sum(jnp.where(hot, tile[local + i : local + i + 1, :], 0.0), axis=1, keepdims=True)
+            slot_grad[i, source] = (gate * held).astype(BF16)
+            inner = jnp.sum(held * out[i, source].astype(F32), axis=1, keepdims=True)
+            dots_out[source, i : i + 1] = jnp.sum(jnp.where(hot, inner, 0.0), axis=0, keepdims=True)
+        return carry
+
+    lax.fori_loop(0, sources, backward, 0)
+    swap = to_exp(1, dots_out, dots_in)
+    start(swap)
+    dots_in[me] = dots_out[me]
+
+    def pass_on(turn):
+        @pl.when((z > 0) & (last - turn > z))
+        def _():
+            arrived(last - turn)
+            acc[last - turn] += inc[last - turn]
+            along(last - turn, 1).start()
+
+        @pl.when((z < last) & (turn < z))
+        def _():
+            arrived(turn)
+            acc[turn] += inc[turn]
+            along(turn, -1).start()
+
+    pass_on(0)
+    finish(swap)
+    for p in range(sources):
+        dots[my_ctx, p * local : (p + 1) * local] = dots_in[p, 0:local]
+    swap = to_ctx(1, dots)
+    start(swap)
+    for turn in range(1, last):
+        pass_on(turn)
+    finish(swap)
+    whole = sum(dots[i] for i in range(1, n_ctx)) + dots[0]
+    dchosen = mask * ((whole - jnp.sum(whole * gates, axis=0, keepdims=True)) / total)
+    dlogits = probs * (dchosen - jnp.sum(chosen * dchosen, axis=0, keepdims=True))
+    partial = dot(dlogits, wide, 1, 0, HIGHEST)
+    cut = width // sources
+    for p in range(sources):
+        rg_out[p] = partial[:, p * cut : (p + 1) * cut]
+    swap = to_exp(2, rg_out, rg_in)
+    start(swap)
+    token_grad[...] = dot(dlogits.T, weight[...], 1, 0, HIGHEST).astype(BF16)
+    rg_in[me] = rg_out[me]
+    finish(swap)
+    rg_all[me] = sum(rg_in[i] for i in range(1, sources)) + rg_in[0]
+    swap = to_exp(3, rg_all.at[me], rg_all, True)
+    start(swap)
+
+    @pl.when(z > 0)
+    def _():
+        arrived(z)
+        acc[z] += inc[z]
+
+    @pl.when(z < last)
+    def _():
+        arrived(chips)
+        acc[z] += inc[chips]
+
+    mixed[...] = acc[z].astype(BF16)
+    finish(swap)
+    router_grad[...] = rg_all[...]
+
+    def sent(chip, carry):
+        to_sibling(chip).wait_send()
+
+        @pl.when(chip != z)
+        def _():
+            along(chip, 1).wait_send()
+
+        for c in range(2):
+            block = 2 * chip + c
+
+            @pl.when(core == c)
+            def _():
+                gather("held", block, sibling)(2).wait_send()
+
+                @pl.when((chip <= z) & (z < last))
+                def _():
+                    gather("held", block, right)(0).wait_send()
+
+                @pl.when((chip >= z) & (z > 0))
+                def _():
+                    gather("held", block, left)(1).wait_send()
+
+        return carry
+
+    lax.fori_loop(0, chips, sent, 0)
+
+
+def fused(n_ctx, sources, tokens, cotangent, routes, router_weight, expert_out):
+    rows, width = tokens.shape
+    local = expert_out.shape[0]
+    capacity = expert_out.shape[1] // sources
+    experts, chips, cut = local * sources, sources // 2, width // sources
+    tile = -(-2 * local // 8) * 8
+    vmem = pl.BlockSpec(memory_space=pltpu.VMEM)
+    dma = pltpu.SemaphoreType.DMA
+    mixed, token_grad, router_grad, slot_grad = pl.pallas_call(
+        functools.partial(kernel, n_ctx, sources),
+        out_shape=(
+            jax.ShapeDtypeStruct((rows, width), BF16),
+            jax.ShapeDtypeStruct((rows, width), BF16),
+            jax.ShapeDtypeStruct((sources, experts, cut), F32),
+            jax.ShapeDtypeStruct((local, sources, capacity, width), BF16),
+        ),
+        in_specs=[vmem] * 5,
+        out_specs=(vmem,) * 4,
+        scratch_shapes=[
+            pltpu.VMEM((sources, rows, width), BF16),
+            pltpu.VMEM((chips, rows, width), F32),
+            pltpu.VMEM((chips, rows, width), F32),
+            pltpu.VMEM((chips, rows, width), F32),
+            pltpu.VMEM((chips + 1, rows, width), F32),
+            pltpu.VMEM((n_ctx, experts, rows), F32),
+            pltpu.VMEM((sources, tile, rows), F32),
+            pltpu.VMEM((sources, tile, rows), F32),
+            pltpu.VMEM((sources, tile, rows), F32),
+            pltpu.VMEM((sources, tile, rows), F32),
+            pltpu.VMEM((n_ctx, experts, rows), F32),
+            pltpu.VMEM((sources, experts, cut), F32),
+            pltpu.VMEM((sources, experts, cut), F32),
+            pltpu.VMEM((sources, experts, cut), F32),
+            dma((3, sources)),
+            dma((sources,)),
+            dma((chips,)),
+            dma((chips,)),
+            dma((chips,)),
+            dma((chips + 1,)),
+            dma((2, n_ctx)),
+            dma((2, n_ctx)),
+            dma((4, sources)),
+            dma((4, sources)),
+        ],
+        compiler_params=pltpu.CompilerParams(
+            collective_id=0, has_side_effects=True, vmem_limit_bytes=48 * 2**20
+        ),
+    )(
+        tokens,
+        cotangent,
+        routes.T,
+        router_weight.T,
+        expert_out.reshape(local, sources, capacity, width),
+    )
+    router_grad = jnp.swapaxes(router_grad, 1, 2).reshape(router_weight.shape)
+    return mixed, token_grad, router_grad, slot_grad.reshape(expert_out.shape)
+
+
 def solution(mesh):
+    n_ctx, sources = mesh.shape["ctx"], mesh.shape["exp"]
+
+    def step(*args):
+        tokens, _, _, _, expert_out = args
+        rows, width = tokens.shape
+        capacity = expert_out.shape[1] // sources
+        small = sources <= 8 and sources % 2 == 0 and n_ctx > 1
+        if small and capacity % 16 == 0 and rows % 128 == 0 and width % (128 * sources) == 0:
+            return fused(n_ctx, sources, *args)
+        return body(*args)
+
     in_specs = (
         P("exp", "ctx"),
         P("exp", "ctx"),
@@ -68,4 +440,4 @@
         P("exp", None, "ctx"),
     )
     out_specs = (P("exp", "ctx"), P("exp", "ctx"), P("ctx", None), P("exp", None, "ctx"))
-    return jax.shard_map(body, mesh=mesh, in_specs=in_specs, out_specs=out_specs, check_vma=False)
+    return jax.shard_map(step, mesh=mesh, in_specs=in_specs, out_specs=out_specs, check_vma=False)

time: 157 us -> 83.5 us (0.53)
  waiting for transfers between devices: 82.2 us -> 0 us
  Pallas kernels: 0 us -> 75.4 us
  blocking collectives: 32 us -> 0 us
  matrix products: 14.6 us -> 0 us
  between operations: 13.8 us -> 0.65 us
  other arithmetic: 6.69 us -> 0 us
  local copies, waits for them, and re-layouts: 3.66 us -> 7.12 us
  starting transfers between devices: 3.45 us -> 0 us
    pallas_call x0 -> x1, Pallas kernels: none -> 75.4 us  [fused(): pl.pallas_call(functools.partial(kernel, n_ctx, sources), out_shape=(jax....]
    psum x1 -> x0, waiting for transfers between devices: 52.9 us -> none  [body(): lax.psum(jnp.dot(tokens_wide.T, dlogits, precision=HIGHEST), 'exp')]
    reduce_scatter x1 -> x0, waiting for transfers between devices: 24.2 us -> none  [body(): mixed = lax.psum_scatter(partial, 'exp', scatter_dimension=0, tiled=False)]
    psum x2 -> x0, blocking collectives: 21.5 us -> none  [the longest x1 11.5 us: body(): lax.psum(jnp.dot(tokens_wide, router_weight, precision=HIGHEST), 'ctx')]
    dot_general x6 -> x0, matrix products: 14.6 us -> none  [the longest x1 5.84 us: body(): partial = jnp.einsum('slct,slcw->stw', weight, out, precision=HIGHEST)]
    all_to_all x1 -> x0, blocking collectives: 10.5 us -> none  [body(): both = lax.all_to_all(both, 'exp', split_axis=0, concat_axis=0, tiled=True)]
    convert_element_type x2 -> x0, other arithmetic: 4.96 us -> none  [the longest x1 3.18 us: body(): slot_grad = (slot_gate[..., None] * gathered).astype(jnp.bfloat16)]
    unnamed x7 -> x11, local copies, waits for them, and re-layouts: 1.65 us -> 6.49 us
  transfers between devices with their start and end apart: 4 -> 0, of which waited for: 4 -> 0; matrix products, arithmetic and copies ran while one was open for 15% -> 0% of each run, Pallas kernels for 0% -> 0%
where the time goes in v2:
time: 83.5 us; the launch traced here: 83.2 us
  Pallas kernels  75.4 us (90%)
  local copies, waits for them, and re-layouts  7.12 us (9%)
    pallas_call x1, Pallas kernels, fused(): pl.pallas_call(functools.partial(kernel, n_ctx, sources), out_shape=(jax....  75.4 us
    unnamed x11, local copies, waits for them, and re-layouts  6.49 us

profile of v2, /device:TPU:0, one launch (start us, length us, event | category | flops | bytes accessed | tf_op | source)
XLA Modules:
  0.0 83.2 jit_solution(4304651792559847336)
XLA Ops:
  0.6 0.0 copy-start
  0.6 0.9 %copy-done = bf16[128,1024]{1,0:T(8,128)(2,1)S(1)} copy-done((bf16[128,1024]{1,0:T(8,128)(2,1)S(1)}, bf16[128,1024]{1,0:T(8,128)(2,1)}, u32[]{:S(2)}) %copy-start) | copy-done | bytes 262168
  1.6 0.0 copy-start.1
  1.6 0.9 %copy-done.1 = bf16[128,1024]{1,0:T(8,128)(2,1)S(1)} copy-done((bf16[128,1024]{1,0:T(8,128)(2,1)S(1)}, bf16[128,1024]{1,0:T(8,128)(2,1)}, u32[]{:S(2)}) %copy-start.1) | copy-done | bytes 262168
  2.5 0.0 copy-start.2
  2.5 0.8 %copy-done.2 = f32[1024,16]{0,1:T(8,128)S(1)} copy-done((f32[1024,16]{0,1:T(8,128)S(1)}, f32[1024,16]{0,1:T(8,128)}, u32[]{:S(2)}) %copy-start.2) | copy-done | bytes 65560
  3.4 0.0 copy-start.3
  3.4 0.7 copy-done.3
  4.1 75.4 %shard_map.84 = (bf16[128,1024]{1,0:T(8,128)(2,1)S(1)}, bf16[128,1024]{1,0:T(8,128)(2,1)S(1)}, f32[8,16,128]{2,1,0:T(8,128)S(1)}, bf16[2,8,96,1024]{3,2,1,0:T(8,128)(2,1)S(1)}) custom-call(bf16[128,1024]{1,0:T(8,128)(2,1)S(1)} %copy-done, bf16[128,1024]{1,0:T(8,128)(2,1)S(1)} %copy-done.1, s32[8,128]{1,0:T(8,128)S(1)} %bitcast.12, f32[16,1024]{1,0:T(8,128)S(1)} %bitcast.11, ...), custom_call_target="tpu_custom_call" | custom-call | tf_op jit(solution)/shard_map/pallas_call | solution.py:373
  79.5 0.6 copy_bitcast_fusion
  80.2 0.7 copy.15
  80.9 0.7 copy.16
  81.6 1.7 %copy.17 = bf16[2,768,1024]{2,1,0:T(8,128)(2,1)} copy(bf16[2,768,1024]{2,1,0:T(8,128)(2,1)S(1)} %bitcast.10) | data formatting | bytes 6291456
Async XLA Ops:
  0.6 1.0 %copy-start = (bf16[128,1024]{1,0:T(8,128)(2,1)S(1)}, bf16[128,1024]{1,0:T(8,128)(2,1)}, u32[]{:S(2)}) copy-start(bf16[128,1024]{1,0:T(8,128)(2,1)} %tokens.1) | copy-start | bytes 786436
  1.6 0.9 %copy-start.1 = (bf16[128,1024]{1,0:T(8,128)(2,1)S(1)}, bf16[128,1024]{1,0:T(8,128)(2,1)}, u32[]{:S(2)}) copy-start(bf16[128,1024]{1,0:T(8,128)(2,1)} %cot.1) | copy-start | bytes 786436
  2.5 0.8 %copy-start.2 = (f32[1024,16]{0,1:T(8,128)S(1)}, f32[1024,16]{0,1:T(8,128)}, u32[]{:S(2)}) copy-start(f32[1024,16]{0,1:T(8,128)} %param.8) | copy-start | bytes 196612
  3.4 0.7 copy-start.3

commit v3 on v2

--- a/solution.py
+++ b/solution.py
@@ -72,16 +72,16 @@
 
 
 def kernel(
-    n_ctx, sources, tokens, cot, routes, weight, out,
+    n_ctx, sources, tokens_hbm, cot, routes_hbm, weight_hbm, out_hbm,
     mixed, token_grad, router_grad, slot_grad,
     cot_all, acc, give, sib, inc, logit, info_out, info, dots_out, dots_in, dots, rg_out, rg_in,
-    rg_all, ag_send, ag_recv, sib_send, sib_recv, line_send, line_recv, ctx_send, ctx_recv,
+    rg_all, tokens, routes, weight, out, in_sem, ag_send, ag_recv, sib_send, sib_recv, line_send, line_recv, ctx_send, ctx_recv,
     exp_send, exp_recv,
 ):
     rows, width = tokens.shape
     local, _, capacity, _ = out.shape
     experts = local * sources
-    chips = sources // 2
+    chips, halves, half = acc.shape[0], acc.shape[1], acc.shape[3]
     last = chips - 1
     me, my_ctx = lax.axis_index("exp"), lax.axis_index("ctx")
     z, core = me // 2, lax.rem(me, 2)
@@ -89,6 +89,21 @@
     sibling = 2 * z + other
     exp_peers = [lax.rem(me + d, sources) for d in range(1, sources)]
     ctx_peers = [lax.rem(my_ctx + d, n_ctx) for d in range(1, n_ctx)]
+
+    loads = [
+        pltpu.make_async_copy(a, b, in_sem.at[i])
+        for i, (a, b) in enumerate(
+            [
+                (tokens_hbm, tokens),
+                (weight_hbm, weight),
+                (routes_hbm, routes),
+                (out_hbm, out),
+                (cot, cot_all.at[me]),
+            ]
+        )
+    ]
+    for load in loads:
+        load.start()
 
     barrier = pltpu.get_barrier_semaphore()
     for p in exp_peers:
@@ -149,6 +164,8 @@
         for c in pair[0]:
             c.wait_send()
 
+    for load in loads[:3]:
+        load.wait()
     wide = tokens[...].astype(F32)
     logit[my_ctx] = dot(weight[...], wide, 1, 1, HIGHEST)
     swap = to_ctx(0, logit)
@@ -174,23 +191,28 @@
     swap = to_exp(0, info_out, info)
     start(swap)
     info[me] = info_out[me]
+    loads[3].wait()
+    loads[4].wait()
     finish(swap)
 
     capacity_iota = lax.broadcasted_iota(jnp.int32, (capacity, rows), 0).astype(F32)
 
+    pair_iota = lax.broadcasted_iota(jnp.int32, (rows, local * capacity), 1).astype(F32)
+
     def part(source):
-        tile = info[source]
+        tile = info[source].T
+        gate = jnp.zeros(pair_iota.shape, F32)
+        for i in range(local):
+            slot_i = tile[:, i : i + 1]
+            place = jnp.where(slot_i >= 0, slot_i + float(i * capacity), -1.0)
+            gate = jnp.where(pair_iota == place, tile[:, local + i : local + i + 1], gate)
+        rows_of = jnp.concatenate([out[i, source] for i in range(local)], axis=0)
         total = None
-        for i in range(local):
-            gate = tile[local + i : local + i + 1, :]
-            rows_of = out[i, source]
-            hot = capacity_iota == tile[i : i + 1, :]
-            for _ in range(3):
-                piece = gate.astype(BF16)
-                gate = gate - piece.astype(F32)
-                put = jnp.where(hot, piece.astype(F32), 0.0).astype(BF16)
-                term = dot(put, rows_of, 0, 0)
-                total = term if total is None else total + term
+        for _ in range(3):
+            piece = gate.astype(BF16)
+            gate = gate - piece.astype(F32)
+            term = dot(piece, rows_of, 1, 0)
+            total = term if total is None else total + term
         return total
 
     def aim(i):
@@ -199,43 +221,51 @@
     def to_sibling(chip):
         return remote(give.at[chip], sib.at[chip], sib_send.at[chip], sib_recv.at[chip], exp=sibling)
 
-    def along(chip, step):
+    def along(chip, h, step):
         to = me + 2 * step
         place = jnp.where((step < 0) & (z - 1 == chip), chips, chip)
-        return remote(acc.at[chip], inc.at[place], line_send.at[chip], line_recv.at[place], exp=to)
-
-    def arrived(place):
-        remote(inc.at[place], inc.at[place], line_send.at[0], line_recv.at[place], exp=sibling).wait_recv()
-
-    def give_away(i, _):
+        return remote(
+            acc.at[chip, h], inc.at[place, h], line_send.at[chip, h], line_recv.at[place, h], exp=to
+        )
+
+    def arrived(place, h):
+        remote(
+            inc.at[place, h], inc.at[place, h], line_send.at[0, h], line_recv.at[place, h], exp=sibling
+        ).wait_recv()
+
+    def first_hop(turn, h):
+        @pl.when(z == 0)
+        def _():
+            along(last - turn, h, 1).start()
+
+        @pl.when(z == last)
+        def _():
+            along(turn, h, -1).start()
+
+    def give_away(i):
         chip = aim(i)
         give[chip] = part(2 * chip + other)
         to_sibling(chip).start()
-        return _
-
-    lax.fori_loop(0, chips, give_away, 0)
-
-    def keep(i, _):
+
+    def keep(i):
         chip = aim(i)
         mine = part(2 * chip + core)
         to_sibling(chip).wait_recv()
-        acc[chip] = mine + sib[chip]
-
-        @pl.when((z == 0) & (chip > z))
-        def _():
-            along(chip, 1).start()
-
-        @pl.when((z == last) & (chip < z))
-        def _():
-            along(chip, -1).start()
-
-        return _
-
-    def keep_loop(i, carry):
-        keep(i, 0)
+        for h in range(halves):
+            cols = slice(h * half, (h + 1) * half)
+            acc[chip, h] = mine[:, cols] + sib[chip, :, cols]
+
+    give_away(0)
+    keep(0)
+    for h in range(halves):
+        first_hop(0, h)
+
+    def give_and_keep(i, carry):
+        give_away(i)
+        keep(i)
         return carry
 
-    lax.fori_loop(0, chips, keep_loop, 0)
+    lax.fori_loop(1, chips, give_and_keep, 0)
 
     for d in range(1, chips):
 
@@ -261,9 +291,36 @@
 
             gather("held", block, sibling)(2).start()
 
-    cot_all[me] = cot[...]
+    def pass_on(turn, h):
+        @pl.when((z > 0) & (last - turn > z))
+        def _():
+            arrived(last - turn, h)
+            acc[last - turn, h] += inc[last - turn, h]
+            along(last - turn, h, 1).start()
+
+        @pl.when((z < last) & (turn < z))
+        def _():
+            arrived(turn, h)
+            acc[turn, h] += inc[turn, h]
+            along(turn, h, -1).start()
 
     def backward(source, carry):
+        turn, h = source // halves, lax.rem(source, halves)
+
+        @pl.when(turn + 1 < last)
+        def _():
+            for step, end, chip in ((1, 0, last - turn), (-1, last, turn)):
+
+                @pl.when(z == end)
+                def _(step=step, chip=chip):
+                    along(chip, h, step).wait_send()
+
+            first_hop(turn + 1, h)
+
+        @pl.when(turn < last)
+        def _():
+            pass_on(turn, h)
+
         @pl.when(lax.rem(source, 2) != core)
         def _():
             gather("held", source, sibling)(2).wait_recv()
@@ -282,28 +339,11 @@
     swap = to_exp(1, dots_out, dots_in)
     start(swap)
     dots_in[me] = dots_out[me]
-
-    def pass_on(turn):
-        @pl.when((z > 0) & (last - turn > z))
-        def _():
-            arrived(last - turn)
-            acc[last - turn] += inc[last - turn]
-            along(last - turn, 1).start()
-
-        @pl.when((z < last) & (turn < z))
-        def _():
-            arrived(turn)
-            acc[turn] += inc[turn]
-            along(turn, -1).start()
-
-    pass_on(0)
     finish(swap)
     for p in range(sources):
         dots[my_ctx, p * local : (p + 1) * local] = dots_in[p, 0:local]
     swap = to_ctx(1, dots)
     start(swap)
-    for turn in range(1, last):
-        pass_on(turn)
     finish(swap)
     whole = sum(dots[i] for i in range(1, n_ctx)) + dots[0]
     dchosen = mask * ((whole - jnp.sum(whole * gates, axis=0, keepdims=True)) / total)
@@ -321,26 +361,32 @@
     swap = to_exp(3, rg_all.at[me], rg_all, True)
     start(swap)
 
-    @pl.when(z > 0)
-    def _():
-        arrived(z)
-        acc[z] += inc[z]
-
-    @pl.when(z < last)
-    def _():
-        arrived(chips)
-        acc[z] += inc[chips]
-
-    mixed[...] = acc[z].astype(BF16)
+    for h in range(halves):
+
+        @pl.when(z > 0)
+        def _(h=h):
+            arrived(z, h)
+            acc[z, h] += inc[z, h]
+
+        @pl.when(z < last)
+        def _(h=h):
+            arrived(chips, h)
+            acc[z, h] += inc[chips, h]
+
+        mixed[:, h * half : (h + 1) * half] = acc[z, h].astype(BF16)
     finish(swap)
     router_grad[...] = rg_all[...]
 
     def sent(chip, carry):
         to_sibling(chip).wait_send()
 
-        @pl.when(chip != z)
-        def _():
-            along(chip, 1).wait_send()
+        hop = jnp.where(z == 0, 1, last - 1)
+        near = ((z > 0) & (z < last)) | (chip == hop)
+
+        @pl.when((chip != z) & near)
+        def _():
+            for h in range(halves):
+                along(chip, h, 1).wait_send()
 
         for c in range(2):
             block = 2 * chip + c
@@ -368,6 +414,7 @@
     capacity = expert_out.shape[1] // sources
     experts, chips, cut = local * sources, sources // 2, width // sources
     tile = -(-2 * local // 8) * 8
+    halves = 2
     vmem = pl.BlockSpec(memory_space=pltpu.VMEM)
     dma = pltpu.SemaphoreType.DMA
     mixed, token_grad, router_grad, slot_grad = pl.pallas_call(
@@ -378,14 +425,14 @@
             jax.ShapeDtypeStruct((sources, experts, cut), F32),
             jax.ShapeDtypeStruct((local, sources, capacity, width), BF16),
         ),
-        in_specs=[vmem] * 5,
+        in_specs=[pl.BlockSpec(memory_space=pltpu.HBM)] * 5,
         out_specs=(vmem,) * 4,
         scratch_shapes=[
             pltpu.VMEM((sources, rows, width), BF16),
+            pltpu.VMEM((chips, halves, rows, width // halves), F32),
             pltpu.VMEM((chips, rows, width), F32),
             pltpu.VMEM((chips, rows, width), F32),
-            pltpu.VMEM((chips, rows, width), F32),
-            pltpu.VMEM((chips + 1, rows, width), F32),
+            pltpu.VMEM((chips + 1, halves, rows, width // halves), F32),
             pltpu.VMEM((n_ctx, experts, rows), F32),
             pltpu.VMEM((sources, tile, rows), F32),
             pltpu.VMEM((sources, tile, rows), F32),
@@ -395,12 +442,17 @@
             pltpu.VMEM((sources, experts, cut), F32),
             pltpu.VMEM((sources, experts, cut), F32),
             pltpu.VMEM((sources, experts, cut), F32),
+            pltpu.VMEM((rows, width), BF16),
+            pltpu.VMEM(routes.shape[::-1], jnp.int32),
+            pltpu.VMEM(router_weight.shape[::-1], F32),
+            pltpu.VMEM((local, sources, capacity, width), BF16),
+            dma((5,)),
             dma((3, sources)),
             dma((sources,)),
             dma((chips,)),
             dma((chips,)),
-            dma((chips,)),
-            dma((chips + 1,)),
+            dma((chips, halves)),
+            dma((chips + 1, halves)),
             dma((2, n_ctx)),
             dma((2, n_ctx)),
             dma((4, sources)),
@@ -427,7 +479,7 @@
         tokens, _, _, _, expert_out = args
         rows, width = tokens.shape
         capacity = expert_out.shape[1] // sources
-        small = sources <= 8 and sources % 2 == 0 and n_ctx > 1
+        small = sources in (4, 6, 8) and n_ctx > 1
         if small and capacity % 16 == 0 and rows % 128 == 0 and width % (128 * sources) == 0:
             return fused(n_ctx, sources, *args)
         return body(*args)

time: 83.5 us -> 89.5 us (1.072)
  Pallas kernels: 75.4 us -> 81.4 us
    pallas_call x1, Pallas kernels: 75.4 us -> 81.4 us  [fused(): pl.pallas_call(functools.partial(kernel, n_ctx, sources), out_shape=(jax....]
where the time goes in v3:
time: 89.5 us; the launch traced here: 89.2 us
  Pallas kernels  81.4 us (91%)
  local copies, waits for them, and re-layouts  7.12 us (8%)
    pallas_call x1, Pallas kernels, fused(): pl.pallas_call(functools.partial(kernel, n_ctx, sources), out_shape=(jax....  81.4 us
    unnamed x11, local copies, waits for them, and re-layouts  6.49 us

profile of v3, /device:TPU:0, one launch (start us, length us, event | category | flops | bytes accessed | tf_op | source)
XLA Modules:
  0.0 89.2 jit_solution(11636611111387270436)
XLA Ops:
  0.6 0.0 copy-start
  0.6 0.9 %copy-done = bf16[128,1024]{1,0:T(8,128)(2,1)S(1)} copy-done((bf16[128,1024]{1,0:T(8,128)(2,1)S(1)}, bf16[128,1024]{1,0:T(8,128)(2,1)}, u32[]{:S(2)}) %copy-start) | copy-done | bytes 262168
  1.6 0.0 copy-start.1
  1.6 0.9 %copy-done.1 = bf16[128,1024]{1,0:T(8,128)(2,1)S(1)} copy-done((bf16[128,1024]{1,0:T(8,128)(2,1)S(1)}, bf16[128,1024]{1,0:T(8,128)(2,1)}, u32[]{:S(2)}) %copy-start.1) | copy-done | bytes 262168
  2.5 0.0 copy-start.2
  2.5 0.8 copy-done.2
  3.4 0.0 copy-start.3
  3.4 0.7 copy-done.3
  4.1 81.4 %shard_map.84 = (bf16[128,1024]{1,0:T(8,128)(2,1)S(1)}, bf16[128,1024]{1,0:T(8,128)(2,1)S(1)}, f32[8,16,128]{2,1,0:T(8,128)S(1)}, bf16[2,8,96,1024]{3,2,1,0:T(8,128)(2,1)S(1)}) custom-call(bf16[128,1024]{1,0:T(8,128)(2,1)S(1)} %copy-done, bf16[128,1024]{1,0:T(8,128)(2,1)S(1)} %copy-done.1, s32[8,128]{1,0:T(8,128)S(1)} %bitcast.12, f32[16,1024]{1,0:T(8,128)S(1)} %bitcast.11, ...), custom_call_target="tpu_custom_call" | custom-call | tf_op jit(solution)/shard_map/pallas_call | solution.py:420
  85.5 0.6 copy_bitcast_fusion
  86.1 0.7 copy.15
  86.8 0.7 copy.16
  87.5 1.7 %copy.17 = bf16[2,768,1024]{2,1,0:T(8,128)(2,1)} copy(bf16[2,768,1024]{2,1,0:T(8,128)(2,1)S(1)} %bitcast.10) | data formatting | bytes 6291456
Async XLA Ops:
  0.6 1.0 %copy-start = (bf16[128,1024]{1,0:T(8,128)(2,1)S(1)}, bf16[128,1024]{1,0:T(8,128)(2,1)}, u32[]{:S(2)}) copy-start(bf16[128,1024]{1,0:T(8,128)(2,1)} %tokens_hbm.1) | copy-start | bytes 786436
  1.6 0.9 %copy-start.1 = (bf16[128,1024]{1,0:T(8,128)(2,1)S(1)}, bf16[128,1024]{1,0:T(8,128)(2,1)}, u32[]{:S(2)}) copy-start(bf16[128,1024]{1,0:T(8,128)(2,1)} %cot.1) | copy-start | bytes 786436
  2.5 0.8 copy-start.2
  3.4 0.7 copy-start.3
